TPU v7x, 32 devices: a whole 2x2x4 slice. The times are simulated.
32 devices in a mesh: groups: 2 (over x), cand: 16 (over z, y, core).
Axes of the slice: x: 2, y: 2, z: 4, core: 2. Of those that a mesh axis runs over, the one named last changes fastest.
Arguments:
- cand_rows: bfloat16 [24576, 1024], P(('groups', 'cand')), parts along dimension 0, may hold values from -6 to 6
- user_rows: bfloat16 [192, 1024], P(('groups', 'cand')), parts along dimension 0, may hold values from -6 to 6
- counts: int32 [192], P(('groups', 'cand')), parts along dimension 0, may hold values from 16 to 512, as said below
- starts: int32 [192], P(('groups', 'cand')), parts along dimension 0, may hold values from 0 to 47, as said below
- norm_gain: float32 [1024], replicated, may hold values from 0.1 to 1.9
- w_cand: bfloat16 [1024, 1024], replicated, may hold values from -0.1875 to 0.1875
- w_user: bfloat16 [1024, 1024], replicated, may hold values from -0.1875 to 0.1875
- w_query: bfloat16 [1024, 1024], replicated, may hold values from -0.25 to 0.25
- w_key: bfloat16 [1024, 1024], replicated, may hold values from -0.25 to 0.25
- w_value: bfloat16 [1024, 1024], replicated, may hold values from -0.1875 to 0.1875
- w_out: bfloat16 [1024, 1024], replicated, may hold values from -0.1875 to 0.1875
- w_score: float32 [1024], replicated, may hold values from -0.1875 to 0.1875
Outputs:
- score: float32 [24576], P(('groups', 'cand')), parts along dimension 0
There are 2 independent parts, one for each index of `groups`. A program takes and returns all parts, laid end to end along the dimension named above; an argument that names none is the same for every part. Nothing has to cross between parts.
Inputs may be any that keep to these rules, and one draw needn't show every extreme that they name: Within a shard the requests' first tiles increase. Each request's tiles run from its first tile to the next request's first tile; for a shard's last request, to the shard's end and then through the next shard's tiles before that shard's first request. On shard 0 the first request starts at tile 0, elsewhere at most 8 tiles in, which some shard reaches; the last shard's last request ends with the shard and starts at its last tile. `counts`: each count is at most the rows of its request's tiles; some request has exactly 512.
All inputs are finite; a program needn't handle non-finite values.
Results may differ from a plain program's by a relative error of at most 0.0045.
Values may be sent and summed in bfloat16 or wider, within the bound.
A program may use at most 128 MiB of HBM per device.

v0:
```python
import jax
import jax.numpy as jnp
from jax import lax
from jax.sharding import PartitionSpec as P

HEADS = 8
TILE = 16
SPILL = 128


def passed_along(block, axis, distance):
    devices = range(lax.axis_size(axis))
    route = [(i - distance, i) for i in devices if i - distance in devices]
    return lax.ppermute(block, axis, route)


def attend(queries, q_labels, key_rows, value_rows, k_labels, head_count):
    head_size = queries.shape[1] // head_count
    allowed = (q_labels[:, None] == k_labels[None, :]) & (q_labels[:, None] >= 0)

    def one_head(head_index):
        col_start = head_index * head_size
        q_part = lax.dynamic_slice_in_dim(queries, col_start, head_size, 1)
        k_part = lax.dynamic_slice_in_dim(key_rows, col_start, head_size, 1)
        v_part = lax.dynamic_slice_in_dim(value_rows, col_start, head_size, 1)
        scores = lax.dot_general(
            q_part, k_part, (((1,), (1,)), ((), ())), preferred_element_type=jnp.float32
        )
        scores = jnp.where(allowed, scores * head_size ** (-0.5), -1e30)
        row_max = jnp.max(scores, axis=1, keepdims=True)
        weights = jnp.exp(scores - row_max)
        row_sum = jnp.sum(weights, axis=1, keepdims=True)
        softmax_weights = (weights / row_sum).astype(jnp.bfloat16)
        return jnp.dot(softmax_weights, v_part, preferred_element_type=jnp.float32).astype(
            jnp.bfloat16
        )

    mixture = lax.map(one_head, jnp.arange(head_count))
    return jnp.transpose(mixture, (1, 0, 2)).reshape(queries.shape[0], head_count * head_size)


def per_device(
    cand_rows,
    user_rows,
    counts,
    starts,
    norm_gain,
    w_cand,
    w_user,
    w_query,
    w_key,
    w_value,
    w_out,
    w_score,
):
    local_rows = cand_rows.shape[0]
    local_reqs = counts.shape[0]
    model_width = cand_rows.shape[1]
    user_term = jnp.dot(user_rows, w_user, preferred_element_type=jnp.float32).astype(jnp.bfloat16)
    first_rows = starts * TILE
    last_first = first_rows[local_reqs - 1]
    last_count = counts[local_reqs - 1]
    bound_pair = jnp.stack([last_first, last_count])
    from_below = passed_along(bound_pair, "cand", 1)
    below_term = passed_along(user_term[local_reqs - 1 :], "cand", 1)
    position = jnp.arange(local_rows, dtype=jnp.int32)
    holder = jnp.sum((position[:, None] >= first_rows[None, :]).astype(jnp.int32), axis=1) - 1
    chosen = holder[:, None] == jnp.arange(local_reqs, dtype=jnp.int32)[None, :]
    row_first = jnp.sum(jnp.where(chosen, first_rows[None, :], 0), axis=1)
    row_count = jnp.sum(jnp.where(chosen, counts[None, :], 0), axis=1)
    usable = jnp.where(
        holder >= 0,
        position - row_first < row_count,
        position + local_rows - from_below[0] < from_below[1],
    )
    labels = jnp.where(usable, holder + 1, -1)
    user_sel = jnp.dot(chosen.astype(jnp.bfloat16), user_term, preferred_element_type=jnp.float32)
    user_sel = user_sel + jnp.where(holder[:, None] < 0, below_term.astype(jnp.float32), 0.0)
    features = cand_rows.astype(jnp.float32)
    mean_square = jnp.mean(features * features, axis=1, keepdims=True)
    normed = (features * lax.rsqrt(mean_square + 1e-06) * norm_gain[None, :]).astype(jnp.bfloat16)
    pre_act = jnp.dot(normed, w_cand, preferred_element_type=jnp.float32) + user_sel
    hidden = (features + jax.nn.silu(pre_act)).astype(jnp.bfloat16)
    queries = jnp.dot(hidden, w_query, preferred_element_type=jnp.float32).astype(jnp.bfloat16)
    key_rows = jnp.dot(hidden, w_key, preferred_element_type=jnp.float32).astype(jnp.bfloat16)
    value_rows = jnp.dot(hidden, w_value, preferred_element_type=jnp.float32).astype(jnp.bfloat16)
    bundle = jnp.concatenate([queries[:SPILL], key_rows[:SPILL], value_rows[:SPILL]], axis=1)
    from_above = passed_along(bundle, "cand", -1)
    offsets = jnp.arange(SPILL, dtype=jnp.int32)
    upper_labels = jnp.where(local_rows + offsets - last_first < last_count, local_reqs, -1)
    all_labels = jnp.concatenate([labels, upper_labels])
    all_queries = jnp.concatenate([queries, from_above[:, :model_width]], axis=0)
    all_keys = jnp.concatenate([key_rows, from_above[:, model_width : 2 * model_width]], axis=0)
    all_values = jnp.concatenate([value_rows, from_above[:, 2 * model_width :]], axis=0)
    mixture_all = attend(all_queries, all_labels, all_keys, all_values, all_labels, HEADS)
    sent_up = passed_along(mixture_all[local_rows:], "cand", 1)
    head_part = jnp.where(holder[:SPILL, None] < 0, sent_up, mixture_all[:SPILL])
    mixture = jnp.concatenate([head_part, mixture_all[SPILL:local_rows]], axis=0)
    mixture = jnp.where(usable[:, None], mixture, jnp.zeros_like(mixture))
    combined = hidden.astype(jnp.float32) + jnp.dot(
        mixture, w_out, preferred_element_type=jnp.float32
    )
    score = jnp.sum(combined * w_score[None, :], axis=1)
    return jnp.where(usable, score, 0.0)


def solution(mesh):
    in_specs = (
        P(("groups", "cand"), None),
        P(("groups", "cand"), None),
        P(("groups", "cand")),
        P(("groups", "cand")),
        P(),
        P(),
        P(),
        P(),
        P(),
        P(),
        P(),
        P(),
    )
    out_specs = P(("groups", "cand"))
    return jax.shard_map(
        per_device, mesh=mesh, in_specs=in_specs, out_specs=out_specs, check_vma=False
    )
```

profile of v0, /device:TPU:24, one launch (start us, length us, event | category | flops | bytes accessed | tf_op | source)
XLA Modules:
  0.0 98.9 jit_solution(7597117351747911509)
XLA Ops:
  0.0 2.2 %convolution_convert_fusion.3 = bf16[6,1024]{1,0:T(8,128)(2,1)S(1)} fusion(bf16[6,1024]{1,0:T(8,128)(2,1)} %param.15, bf16[1024,1024]{1,0:T(8,128)(2,1)} %param.20), kind=kOutput, calls=%fused_computation.35 | convolution fusion | flops 12589056 | bytes 2121728 | tf_op jit(solution)/shard_map/dot_general | solution.py:59
  2.2 2.1 %collective-permute-start.1 = (bf16[1,1024]{1,0:T(2,128)(2,1)S(1)}, bf16[1,1024]{1,0:T(2,128)(2,1)S(1)}, u32[]{:S(2)}, u32[]{:S(2)}) collective-permute-start(bf16[1,1024]{1,0:T(2,128)(2,1)S(1)} %slice.72), channel_id=1, source_target_pairs={{0,1},{1,2},{2,3},{3,4},{4,5},{5,6},{6,7},{7,8},{8,9},{9,10},{10,1... | collective-permute-start | bytes 6152 | tf_op jit(solution)/shard_map/ppermute | solution.py:14
  8.2 3.0 %fusion.14 = bf16[768,1024]{1,0:T(8,128)(2,1)S(1)} fusion(bf16[768,1024]{1,0:T(8,128)(2,1)S(1)} %copy-done.7, f32[768,1024]{1,0:T(8,128)S(1)} %fusion.25, f32[1024]{0:T(1024)S(1)} %bitcast.32, bf16[1024,1024]{1,0:T(8,128)(2,1)S(1)} %copy-done, f32[1024]{0:T(1024)S(1)} %copy-done.13, f32[768]{0:T(1024)S(1)} %add_rsqrt_fusion, ...), kind=kOutput, calls=%fused_computation.20 | convolution fusion | flops 1621622784 | bytes 8400640 | tf_op jit(solution)/shard_map/dot_general | solution.py:82
  11.2 1.8 %convolution_convert_fusion.2 = bf16[768,1024]{1,0:T(8,128)(2,1)S(1)} fusion(bf16[768,1024]{1,0:T(8,128)(2,1)S(1)} %fusion.14, bf16[1024,1024]{1,0:T(8,128)(2,1)S(1)} %copy-done.9), kind=kOutput, calls=%fused_computation.27 | convolution fusion | flops 1611399168 | bytes 5242880 | tf_op jit(solution)/shard_map/dot_general | solution.py:84
  13.3 1.8 %convolution_convert_fusion.1 = bf16[768,1024]{1,0:T(8,128)(2,1)S(1)} fusion(bf16[768,1024]{1,0:T(8,128)(2,1)S(1)} %fusion.14, bf16[1024,1024]{1,0:T(8,128)(2,1)S(1)} %copy-done.10), kind=kOutput, calls=%fused_computation.26 | convolution fusion | flops 1611399168 | bytes 5242880 | tf_op jit(solution)/shard_map/dot_general | solution.py:85
  15.2 1.8 %convolution_convert_fusion = bf16[768,1024]{1,0:T(8,128)(2,1)S(1)} fusion(bf16[768,1024]{1,0:T(8,128)(2,1)S(1)} %fusion.14, bf16[1024,1024]{1,0:T(8,128)(2,1)S(1)} %copy-done.11), kind=kOutput, calls=%fused_computation.25 | convolution fusion | flops 1611399168 | bytes 5242880 | tf_op jit(solution)/shard_map/dot_general | solution.py:86
  18.6 3.1 %collective-permute-start.2 = (bf16[128,3072]{1,0:T(8,128)(2,1)}, bf16[128,3072]{1,0:T(8,128)(2,1)S(1)}, u32[]{:S(2)}, u32[]{:S(2)}) collective-permute-start(bf16[128,3072]{1,0:T(8,128)(2,1)} %pad_maximum_fusion.3), channel_id=1, source_target_pairs={{1,0},{2,1},{3,2},{4,3},{5,4},{6,5},{7,6},{8,7},{9,8},{10,9},{11,1... | collective-permute-start | bytes 2359304 | tf_op jit(solution)/shard_map/ppermute | solution.py:14
  23.0 1.9 %collective-permute-start = (s32[2]{0:T(128)S(1)}, s32[2]{0:T(128)S(1)}, u32[]{:S(2)}, u32[]{:S(2)}) collective-permute-start(s32[2]{0:T(128)S(1)} %pad_add_fusion.1), channel_id=1, source_target_pairs={{0,1},{1,2},{2,3},{3,4},{4,5},{5,6},{6,7},{7,8},{8,9},{9,10},{10,1... | collective-permute-start | bytes 32 | tf_op jit(solution)/shard_map/ppermute | solution.py:14
  26.5 2.3 %collective-permute-done = s32[2]{0:T(128)S(1)} collective-permute-done((s32[2]{0:T(128)S(1)}, s32[2]{0:T(128)S(1)}, u32[]{:S(2)}, u32[]{:S(2)}) %collective-permute-start) | collective-permute-done | bytes 40 | tf_op jit(solution)/shard_map/ppermute | solution.py:14
  34.1 2.2 %pad_maximum_fusion = (bf16[896,1024]{1,0:T(8,128)(2,1)}, bf16[896,1024]{1,0:T(8,128)(2,1)}) fusion(bf16[128,1024]{1,0:T(8,128)(2,1)S(1)} %get-tuple-element.91, bf16[768,1024]{1,0:T(8,128)(2,1)S(1)} %copy-done.2, bf16[128,1024]{1,0:T(8,128)(2,1)S(1)} %get-tuple-element.90, bf16[768,1024]{1,0:T(8,128)(2,1)S(1)} %copy-done.4), kind=kLoop, calls=%fused_computation.22 | loop fusion | flops 7340032 | bytes 7340032 | tf_op jit(solution)/shard_map/concatenate | solution.py:92
  36.3 49.7 %while.11 = (s32[]{:T(128)}, bf16[8,896,128]{1,2,0:T(8,128)(2,1)}, s32[8]{0:T(128)S(1)}, bf16[896,1024]{1,0:T(8,128)(2,1)}, bf16[896,1024]{1,0:T(8,128)(2,1)}, /...) while((s32[]{:T(128)}, bf16[8,896,128]{1,2,0:T(8,128)(2,1)}, ...), condition=%wide.region_7.8_spmd.clone, body=%wide.region_4.7_spmd.clone.sunk | while | flops 419182848 | bytes 11497651 | solution.py:38
  37.6 2.0 %fusion.51 = (f32[896]{0:T(1024)S(1)}, f32[896,896]{0,1:T(8,128)S(1)}) fusion(bf16[896,1024]{1,0:T(8,128)(2,1)} %get-tuple-element.177, s32[]{:T(128)S(6)} %select_n.78, bf16[896,1024]{1,0:T(8,128)(2,1)} %get-tuple-element.176, pred[896]{0:T(1024)(128)(4,1)S(1)} %get-tuple-element.180, s32[896]{0:T(1024)S(1)} %get-tuple-element.179), kind=kOutput, calls=%fused_computation.62.clone.1 | convolution fusion | flops 209534080 | bytes 3683840 | tf_op jit(solution)/shard_map/while/body/eval_jaxpr/dot_general | solution.py:26
  40.0 1.6 %fusion.53 = bf16[1,896,128]{2,1,0:T(8,128)(2,1)S(1)} fusion(f32[896,896]{0,1:T(8,128)S(1)} %get-tuple-element.147, f32[896]{0:T(1024)S(1)} %fusion.52, f32[896]{0:T(1024)S(1)} %get-tuple-element.148, bf16[896,1024]{1,0:T(8,128)(2,1)} %get-tuple-element.178, s32[]{:T(128)S(6)} %select_n.78), kind=kOutput, calls=%fused_computation.7.clone.1 | convolution fusion | flops 208044032 | bytes 3677188 | tf_op jit(solution)/shard_map/while/body/eval_jaxpr/dot_general | solution.py:34
  43.8 2.0 %fusion.51 = (f32[896]{0:T(1024)S(1)}, f32[896,896]{0,1:T(8,128)S(1)}) fusion(bf16[896,1024]{1,0:T(8,128)(2,1)} %get-tuple-element.177, s32[]{:T(128)S(6)} %select_n.78, bf16[896,1024]{1,0:T(8,128)(2,1)} %get-tuple-element.176, pred[896]{0:T(1024)(128)(4,1)S(1)} %get-tuple-element.180, s32[896]{0:T(1024)S(1)} %get-tuple-element.179), kind=kOutput, calls=%fused_computation.62.clone.1 | convolution fusion | flops 209534080 | bytes 3683840 | tf_op jit(solution)/shard_map/while/body/eval_jaxpr/dot_general | solution.py:26
  50.0 2.0 %fusion.51 = (f32[896]{0:T(1024)S(1)}, f32[896,896]{0,1:T(8,128)S(1)}) fusion(bf16[896,1024]{1,0:T(8,128)(2,1)} %get-tuple-element.177, s32[]{:T(128)S(6)} %select_n.78, bf16[896,1024]{1,0:T(8,128)(2,1)} %get-tuple-element.176, pred[896]{0:T(1024)(128)(4,1)S(1)} %get-tuple-element.180, s32[896]{0:T(1024)S(1)} %get-tuple-element.179), kind=kOutput, calls=%fused_computation.62.clone.1 | convolution fusion | flops 209534080 | bytes 3683840 | tf_op jit(solution)/shard_map/while/body/eval_jaxpr/dot_general | solution.py:26
  56.2 2.0 %fusion.51 = (f32[896]{0:T(1024)S(1)}, f32[896,896]{0,1:T(8,128)S(1)}) fusion(bf16[896,1024]{1,0:T(8,128)(2,1)} %get-tuple-element.177, s32[]{:T(128)S(6)} %select_n.78, bf16[896,1024]{1,0:T(8,128)(2,1)} %get-tuple-element.176, pred[896]{0:T(1024)(128)(4,1)S(1)} %get-tuple-element.180, s32[896]{0:T(1024)S(1)} %get-tuple-element.179), kind=kOutput, calls=%fused_computation.62.clone.1 | convolution fusion | flops 209534080 | bytes 3683840 | tf_op jit(solution)/shard_map/while/body/eval_jaxpr/dot_general | solution.py:26
  62.4 2.0 %fusion.51 = (f32[896]{0:T(1024)S(1)}, f32[896,896]{0,1:T(8,128)S(1)}) fusion(bf16[896,1024]{1,0:T(8,128)(2,1)} %get-tuple-element.177, s32[]{:T(128)S(6)} %select_n.78, bf16[896,1024]{1,0:T(8,128)(2,1)} %get-tuple-element.176, pred[896]{0:T(1024)(128)(4,1)S(1)} %get-tuple-element.180, s32[896]{0:T(1024)S(1)} %get-tuple-element.179), kind=kOutput, calls=%fused_computation.62.clone.1 | convolution fusion | flops 209534080 | bytes 3683840 | tf_op jit(solution)/shard_map/while/body/eval_jaxpr/dot_general | solution.py:26
  64.9 1.6 %fusion.53 = bf16[1,896,128]{2,1,0:T(8,128)(2,1)S(1)} fusion(f32[896,896]{0,1:T(8,128)S(1)} %get-tuple-element.147, f32[896]{0:T(1024)S(1)} %fusion.52, f32[896]{0:T(1024)S(1)} %get-tuple-element.148, bf16[896,1024]{1,0:T(8,128)(2,1)} %get-tuple-element.178, s32[]{:T(128)S(6)} %select_n.78), kind=kOutput, calls=%fused_computation.7.clone.1 | convolution fusion | flops 208044032 | bytes 3677188 | tf_op jit(solution)/shard_map/while/body/eval_jaxpr/dot_general | solution.py:34
  68.6 2.0 %fusion.51 = (f32[896]{0:T(1024)S(1)}, f32[896,896]{0,1:T(8,128)S(1)}) fusion(bf16[896,1024]{1,0:T(8,128)(2,1)} %get-tuple-element.177, s32[]{:T(128)S(6)} %select_n.78, bf16[896,1024]{1,0:T(8,128)(2,1)} %get-tuple-element.176, pred[896]{0:T(1024)(128)(4,1)S(1)} %get-tuple-element.180, s32[896]{0:T(1024)S(1)} %get-tuple-element.179), kind=kOutput, calls=%fused_computation.62.clone.1 | convolution fusion | flops 209534080 | bytes 3683840 | tf_op jit(solution)/shard_map/while/body/eval_jaxpr/dot_general | solution.py:26
  74.9 2.0 %fusion.51 = (f32[896]{0:T(1024)S(1)}, f32[896,896]{0,1:T(8,128)S(1)}) fusion(bf16[896,1024]{1,0:T(8,128)(2,1)} %get-tuple-element.177, s32[]{:T(128)S(6)} %select_n.78, bf16[896,1024]{1,0:T(8,128)(2,1)} %get-tuple-element.176, pred[896]{0:T(1024)(128)(4,1)S(1)} %get-tuple-element.180, s32[896]{0:T(1024)S(1)} %get-tuple-element.179), kind=kOutput, calls=%fused_computation.62.clone.1 | convolution fusion | flops 209534080 | bytes 3683840 | tf_op jit(solution)/shard_map/while/body/eval_jaxpr/dot_general | solution.py:26
  81.1 2.0 %fusion.51 = (f32[896]{0:T(1024)S(1)}, f32[896,896]{0,1:T(8,128)S(1)}) fusion(bf16[896,1024]{1,0:T(8,128)(2,1)} %get-tuple-element.177, s32[]{:T(128)S(6)} %select_n.78, bf16[896,1024]{1,0:T(8,128)(2,1)} %get-tuple-element.176, pred[896]{0:T(1024)(128)(4,1)S(1)} %get-tuple-element.180, s32[896]{0:T(1024)S(1)} %get-tuple-element.179), kind=kOutput, calls=%fused_computation.62.clone.1 | convolution fusion | flops 209534080 | bytes 3683840 | tf_op jit(solution)/shard_map/while/body/eval_jaxpr/dot_general | solution.py:26
  87.3 2.8 %collective-permute-start.3 = (bf16[128,1024]{0,1:T(8,128)(2,1)S(1)}, bf16[128,1024]{0,1:T(8,128)(2,1)S(1)}, u32[]{:S(2)}, u32[]{:S(2)}) collective-permute-start(bf16[128,1024]{0,1:T(8,128)(2,1)S(1)} %bitcast.31), channel_id=1, source_target_pairs={{0,1},{1,2},{2,3},{3,4},{4,5},{5,6},{6,7},{7,8},{8,9},{9,10},{10,1... | collective-permute-start | bytes 786440 | tf_op jit(solution)/shard_map/ppermute | solution.py:14
  91.6 4.5 %collective-permute-done.3 = bf16[128,1024]{0,1:T(8,128)(2,1)S(1)} collective-permute-done((bf16[128,1024]{0,1:T(8,128)(2,1)S(1)}, bf16[128,1024]{0,1:T(8,128)(2,1)S(1)}, u32[]{:S(2)}, u32[]{:S(2)}) %collective-permute-start.3) | collective-permute-done | bytes 262176 | tf_op jit(solution)/shard_map/ppermute | solution.py:14
  96.2 2.1 %multiply_reduce_fusion = f32[768]{0:T(1024)S(1)} fusion(bf16[768,1024]{1,0:T(8,128)(2,1)S(1)} %copy-done.17, bf16[1024,1024]{1,0:T(8,128)(2,1)S(1)} %copy-done.12, bf16[640,1024]{0,1:T(8,128)(2,1)S(1)} %bitcast.30, bf16[128,1024]{0,1:T(8,128)(2,1)S(1)} %broadcast_select_fusion, f32[1024]{0:T(1024)S(1)} %copy-done.14, pred[768]{0:T(1024)(128)(4,1)S(1)} %get-tuple-element.84), kind=kOutput, calls=%fused_computation.21 | convolution fusion | flops 1617689856 | bytes 5250816 | tf_op jit(solution)/shard_map/dot_general | solution.py:100
  (107 shorter events, 42.7 us)
Async XLA Ops:
  0.0 8.1 %copy-start = (bf16[1024,1024]{1,0:T(8,128)(2,1)S(1)}, bf16[1024,1024]{1,0:T(8,128)(2,1)}, u32[]{:S(2)}) copy-start(bf16[1024,1024]{1,0:T(8,128)(2,1)} %param.19) | copy-start | bytes 6291460
  0.0 4.2 %copy-start.15 = (s32[6]{0:T(128)S(1)}, s32[6]{0:T(128)}, u32[]{:S(2)}) copy-start(s32[6]{0:T(128)} %param.17) | copy-start | bytes 76
  2.2 2.9 %copy-start.7 = (bf16[768,1024]{1,0:T(8,128)(2,1)S(1)}, bf16[768,1024]{1,0:T(8,128)(2,1)}, u32[]{:S(2)}) copy-start(bf16[768,1024]{1,0:T(8,128)(2,1)} %param.14) | copy-start | bytes 4718596
  2.2 6.0 %collective-permute-start.1 = (bf16[1,1024]{1,0:T(2,128)(2,1)S(1)}, bf16[1,1024]{1,0:T(2,128)(2,1)S(1)}, u32[]{:S(2)}, u32[]{:S(2)}) collective-permute-start(bf16[1,1024]{1,0:T(2,128)(2,1)S(1)} %slice.72), channel_id=1, source_target_pairs={{0,1},{1,2},{2,3},{3,4},{4,5},{5,6},{6,7},{7,8},{8,9},{9,10},{10,1... | collective-permute-start | bytes 6152 | tf_op jit(solution)/shard_map/ppermute | solution.py:14
  4.4 1.7 %copy-start.8 = (s32[6]{0:T(128)S(1)}, s32[6]{0:T(128)}, u32[]{:S(2)}) copy-start(s32[6]{0:T(128)} %param.16) | copy-start | bytes 76
  4.4 3.8 %copy-start.13 = (f32[1024]{0:T(1024)S(1)}, f32[1024]{0:T(1024)}, u32[]{:S(2)}) copy-start(f32[1024]{0:T(1024)} %param.18) | copy-start | bytes 12292
  8.2 3.0 %copy-start.9 = (bf16[1024,1024]{1,0:T(8,128)(2,1)S(1)}, bf16[1024,1024]{1,0:T(8,128)(2,1)}, u32[]{:S(2)}) copy-start(bf16[1024,1024]{1,0:T(8,128)(2,1)} %param.21) | copy-start | bytes 6291460
  11.2 4.0 %copy-start.16 = (bf16[768,1024]{1,0:T(8,128)(2,1)}, bf16[768,1024]{1,0:T(8,128)(2,1)S(1)}, u32[]{:S(2)}) copy-start(bf16[768,1024]{1,0:T(8,128)(2,1)S(1)} %fusion.14) | copy-start | bytes 4718596
  11.2 2.2 %copy-start.10 = (bf16[1024,1024]{1,0:T(8,128)(2,1)S(1)}, bf16[1024,1024]{1,0:T(8,128)(2,1)}, u32[]{:S(2)}) copy-start(bf16[1024,1024]{1,0:T(8,128)(2,1)} %param.22) | copy-start | bytes 6291460
  13.0 2.2 %copy-start.1 = (bf16[768,1024]{1,0:T(8,128)(2,1)}, bf16[768,1024]{1,0:T(8,128)(2,1)S(1)}, u32[]{:S(2)}) copy-start(bf16[768,1024]{1,0:T(8,128)(2,1)S(1)} %convolution_convert_fusion.2) | copy-start | bytes 4718596
  13.3 1.9 %copy-start.11 = (bf16[1024,1024]{1,0:T(8,128)(2,1)S(1)}, bf16[1024,1024]{1,0:T(8,128)(2,1)}, u32[]{:S(2)}) copy-start(bf16[1024,1024]{1,0:T(8,128)(2,1)} %param.23) | copy-start | bytes 6291460
  15.2 1.9 %copy-start.3 = (bf16[768,1024]{1,0:T(8,128)(2,1)}, bf16[768,1024]{1,0:T(8,128)(2,1)S(1)}, u32[]{:S(2)}) copy-start(bf16[768,1024]{1,0:T(8,128)(2,1)S(1)} %convolution_convert_fusion.1) | copy-start | bytes 4718596
  15.2 1.9 %slice-start = ((bf16[768,1024]{1,0:T(8,128)(2,1)}), bf16[128,1024]{1,0:T(8,128)(2,1)S(1)}, s32[]{:S(2)}) async-start(bf16[768,1024]{1,0:T(8,128)(2,1)} %copy-done.1), calls=%async_computation | async-start | bytes 524288 | tf_op jit(solution)/shard_map/slice | solution.py:87
  17.1 1.5 %copy-start.5 = (bf16[768,1024]{1,0:T(8,128)(2,1)}, bf16[768,1024]{1,0:T(8,128)(2,1)S(1)}, u32[]{:S(2)}) copy-start(bf16[768,1024]{1,0:T(8,128)(2,1)S(1)} %convolution_convert_fusion) | copy-start | bytes 4718596
  18.6 12.9 %collective-permute-start.2 = (bf16[128,3072]{1,0:T(8,128)(2,1)}, bf16[128,3072]{1,0:T(8,128)(2,1)S(1)}, u32[]{:S(2)}, u32[]{:S(2)}) collective-permute-start(bf16[128,3072]{1,0:T(8,128)(2,1)} %pad_maximum_fusion.3), channel_id=1, source_target_pairs={{1,0},{2,1},{3,2},{4,3},{5,4},{6,5},{7,6},{8,7},{9,8},{10,9},{11,1... | collective-permute-start | bytes 2359304 | tf_op jit(solution)/shard_map/ppermute | solution.py:14
  23.0 5.7 %collective-permute-start = (s32[2]{0:T(128)S(1)}, s32[2]{0:T(128)S(1)}, u32[]{:S(2)}, u32[]{:S(2)}) collective-permute-start(s32[2]{0:T(128)S(1)} %pad_add_fusion.1), channel_id=1, source_target_pairs={{0,1},{1,2},{2,3},{3,4},{4,5},{5,6},{6,7},{7,8},{8,9},{9,10},{10,1... | collective-permute-start | bytes 32 | tf_op jit(solution)/shard_map/ppermute | solution.py:14
  25.0 6.6 %copy-start.6 = (bf16[768,1024]{1,0:T(8,128)(2,1)S(1)}, bf16[768,1024]{1,0:T(8,128)(2,1)}, u32[]{:S(2)}) copy-start(bf16[768,1024]{1,0:T(8,128)(2,1)} %copy-done.5) | copy-start | bytes 4718596
  31.5 2.1 %copy-start.2 = (bf16[768,1024]{1,0:T(8,128)(2,1)S(1)}, bf16[768,1024]{1,0:T(8,128)(2,1)}, u32[]{:S(2)}) copy-start(bf16[768,1024]{1,0:T(8,128)(2,1)} %copy-done.1) | copy-start | bytes 4718596
  31.6 2.5 %copy-start.4 = (bf16[768,1024]{1,0:T(8,128)(2,1)S(1)}, bf16[768,1024]{1,0:T(8,128)(2,1)}, u32[]{:S(2)}) copy-start(bf16[768,1024]{1,0:T(8,128)(2,1)} %copy-done.3) | copy-start | bytes 4718596
  86.1 10.1 %copy-start.12 = (bf16[1024,1024]{1,0:T(8,128)(2,1)S(1)}, bf16[1024,1024]{1,0:T(8,128)(2,1)}, u32[]{:S(2)}) copy-start(bf16[1024,1024]{1,0:T(8,128)(2,1)} %param.24) | copy-start | bytes 6291460
  86.1 10.1 %copy-start.14 = (f32[1024]{0:T(1024)S(1)}, f32[1024]{0:T(1024)}, u32[]{:S(2)}) copy-start(f32[1024]{0:T(1024)} %param.25) | copy-start | bytes 12292
  86.1 10.1 %copy-start.17 = (bf16[768,1024]{1,0:T(8,128)(2,1)S(1)}, bf16[768,1024]{1,0:T(8,128)(2,1)}, u32[]{:S(2)}) copy-start(bf16[768,1024]{1,0:T(8,128)(2,1)} %copy-done.16) | copy-start | bytes 4718596
  87.3 8.8 %collective-permute-start.3 = (bf16[128,1024]{0,1:T(8,128)(2,1)S(1)}, bf16[128,1024]{0,1:T(8,128)(2,1)S(1)}, u32[]{:S(2)}, u32[]{:S(2)}) collective-permute-start(bf16[128,1024]{0,1:T(8,128)(2,1)S(1)} %bitcast.31), channel_id=1, source_target_pairs={{0,1},{1,2},{2,3},{3,4},{4,5},{5,6},{6,7},{7,8},{8,9},{9,10},{10,1... | collective-permute-start | bytes 786440 | tf_op jit(solution)/shard_map/ppermute | solution.py:14
where the time goes:
time: 99.7 us; the launch traced here: 98.9 us
  matrix products  42 us (42%)
  local copies, waits for them, and re-layouts  18.3 us (18%)
  other arithmetic  13.9 us (14%)
  starting transfers between devices  9.87 us (10%)
  waiting for transfers between devices  9.05 us (9%)
  loops' own time  5.36 us (5%)
    dot_general x8, matrix products, one_head(): lax.dot_general(q_part, k_part, (((1,), (1,)), ((), ())), preferred_eleme...  15.6 us
    dot_general x8, matrix products, one_head(): jnp.dot(softmax_weights, v_part, preferred_element_type=jnp.float32)  13.1 us
    ppermute x4, starting transfers between devices, passed_along(): return lax.ppermute(block, axis, route)  9.87 us
    ppermute x4, waiting for transfers between devices, passed_along(): return lax.ppermute(block, axis, route)  9.05 us
    dynamic_update_slice x16, local copies, waits for them, and re-layouts, attend(): mixture = lax.map(one_head, jnp.arange(head_count))  7.1 us
    another operation x1, loops' own time, attend(): mixture = lax.map(one_head, jnp.arange(head_count))  5.36 us
    dynamic_slice x8, local copies, waits for them, and re-layouts, attend(): mixture = lax.map(one_head, jnp.arange(head_count))  4.66 us
    reduce_sum x8, other arithmetic, one_head(): row_sum = jnp.sum(weights, axis=1, keepdims=True)  3.91 us
  transfers between devices with their start and end apart: 4, of which 4 were waited for; matrix products, arithmetic and copies ran while one was open for 9% of the time, Pallas kernels for 0%

commit v1 on v0

v1 whole, which is shorter than its diff:
```python
import functools
import math

import jax
import jax.numpy as jnp
from jax import lax
from jax.experimental import pallas as pl
from jax.experimental.pallas import tpu as pltpu
from jax.sharding import PartitionSpec as P

HEADS = 8
TILE = 16
SPILL = 128
MAXC = 512
LANES = 128
FAR = -1e30
LOW = 16
MESH = pl.DeviceIdType.MESH


def dot(a, b):
    return jnp.dot(a, b, preferred_element_type=jnp.float32)


def dot_t(a, b):
    return lax.dot_general(
        a, b, (((1,), (1,)), ((), ())), preferred_element_type=jnp.float32
    )


def parts_of(value):
    high = value.astype(jnp.bfloat16)
    return high, (value - high.astype(jnp.float32)).astype(jnp.bfloat16)


def fold_lanes(value):
    total = value[:, :LANES]
    for at in range(LANES, value.shape[1], LANES):
        total = total + value[:, at : at + LANES]
    return total


def kernel(
    shards,
    starts,
    counts,
    x_hbm,
    users,
    gain,
    w_score,
    w_user_hbm,
    w_cand_hbm,
    w_out_hbm,
    w_value_hbm,
    w_query_hbm,
    w_key_hbm,
    out,
    x_own,
    x_next,
    w_user,
    w_cand,
    w_out,
    w_value,
    w_query,
    w_key,
    terms,
    hidden,
    queries,
    keys,
    q_mark,
    k_mark,
    sides,
    total,
    score_out,
    score_in,
    load_sem,
    send_sem,
    recv_sem,
):
    local, width = x_own.shape
    reqs = starts.shape[0]
    head_size = width // HEADS
    rows_all = local + SPILL
    me = lax.axis_index("cand")
    has_lower = me > 0
    has_upper = me < shards - 1

    loads = []
    pairs = (
        (x_hbm, x_own),
        (w_user_hbm, w_user),
        (w_cand_hbm, w_cand),
        (w_out_hbm, w_out),
        (w_value_hbm, w_value),
        (w_query_hbm, w_query),
        (w_key_hbm, w_key),
    )
    for at, (src, dst) in enumerate(pairs):
        copy = pltpu.make_async_copy(src, dst, load_sem.at[at])
        copy.start()
        loads.append(copy)

    barrier = pltpu.get_barrier_semaphore()

    @pl.when(has_lower)
    def _():
        pl.semaphore_signal(barrier, inc=1, device_id={"cand": me - 1}, device_id_type=MESH)

    @pl.when(has_upper)
    def _():
        pl.semaphore_signal(barrier, inc=1, device_id={"cand": me + 1}, device_id_type=MESH)

    def rows_down():
        return pltpu.make_async_remote_copy(
            src_ref=x_hbm.at[pl.ds(0, SPILL)],
            dst_ref=x_next,
            send_sem=send_sem.at[0],
            recv_sem=recv_sem.at[0],
            device_id={"cand": me - 1},
            device_id_type=MESH,
        )

    def score_up():
        return pltpu.make_async_remote_copy(
            src_ref=score_out,
            dst_ref=score_in,
            send_sem=send_sem.at[1],
            recv_sem=recv_sem.at[1],
            device_id={"cand": me + 1},
            device_id_type=MESH,
        )

    lane = lax.broadcasted_iota(jnp.int32, (1, LANES), 1)
    first = jnp.full((1, LANES), 1 << 28, jnp.int32)
    after = jnp.full((1, LANES), 1 << 28, jnp.int32)
    live_end = jnp.zeros((1, LANES), jnp.int32)
    for j in range(reqs):
        row = starts[j] * TILE
        first = jnp.where(lane == j, row, first)
        live_end = jnp.where(lane == j, row + counts[j], live_end)
        if j:
            after = jnp.where(lane == j - 1, row, after)

    def marks(base, rows):
        place = base + lax.broadcasted_iota(jnp.int32, (rows, LANES), 0)
        held = (place >= first) & (place < after)
        live = (place >= first) & (place < live_end)
        return held, live

    for base in range(0, rows_all, SPILL):
        _, live = marks(base, SPILL)
        live_f = jnp.where(live, 1.0, 0.0)
        dead = 1.0 - jnp.sum(live_f, axis=1, keepdims=True)
        q_mark[pl.ds(base, SPILL), :] = jnp.where(live, 0.0, FAR).astype(jnp.bfloat16)
        k_mark[pl.ds(base, SPILL), :] = jnp.where(
            lane == LANES - 1, dead, live_f
        ).astype(jnp.bfloat16)

    terms[...] = jnp.zeros_like(terms)
    loads[1].wait()
    terms[0:reqs, :] = dot(users[...], w_user[...])

    both = jnp.where(has_lower, 1, 0) + jnp.where(has_upper, 1, 0)
    pl.semaphore_wait(barrier, both)

    @pl.when(has_lower)
    def _():
        rows_down().start()

    @pl.when(jnp.logical_not(has_upper))
    def _():
        x_next[...] = jnp.zeros_like(x_next)

    @pl.when(jnp.logical_not(has_lower))
    def _():
        score_in[...] = jnp.zeros_like(score_in)

    def pointwise(base, rows, x):
        features = x.astype(jnp.float32)
        mean_square = jnp.mean(features * features, axis=1, keepdims=True)
        normed = (features * lax.rsqrt(mean_square + 1e-06) * gain[...]).astype(jnp.bfloat16)
        held, _ = marks(base, rows)
        user = dot(jnp.where(held, 1.0, 0.0).astype(jnp.bfloat16), terms[...].astype(jnp.bfloat16))
        pre = dot(normed, w_cand[...]) + user
        silu = pre * (0.5 + 0.5 * jnp.tanh(0.5 * pre))
        hidden[pl.ds(base, rows), :] = (features + silu).astype(jnp.bfloat16)

    loads[0].wait()
    loads[2].wait()
    step = 2 * SPILL
    for base in range(0, local, step):
        pointwise(base, step, x_own[pl.ds(base, step), :])

    loads[3].wait()
    loads[4].wait()
    score_high, rest = parts_of(w_score[...])
    score_mid, score_low = parts_of(w_score[...] - score_high.astype(jnp.float32))
    row_id = lax.broadcasted_iota(jnp.int32, (LANES, width), 0)
    spread = jnp.where(
        row_id == 0,
        score_high.astype(jnp.float32),
        jnp.where(
            row_id == 1,
            score_mid.astype(jnp.float32),
            jnp.where(row_id == 2, score_low.astype(jnp.float32), 0.0),
        ),
    ).astype(jnp.bfloat16)
    u = jnp.sum(dot_t(w_out[...], spread), axis=1, keepdims=True)
    u_high = u.astype(jnp.bfloat16).astype(jnp.float32)
    u_low = u - u_high
    head_of = lax.broadcasted_iota(jnp.int32, (width, LANES), 0) // head_size
    lane_w = lax.broadcasted_iota(jnp.int32, (width, LANES), 1)
    by_head = jnp.where(
        lane_w == head_of, u_high, jnp.where(lane_w == head_of + LOW, u_low, 0.0)
    ).astype(jnp.bfloat16)
    g = dot(w_value[...], by_head)
    g = jnp.where(lane < HEADS, g + pltpu.roll(g, LANES - LOW, 1), 0.0)
    g_high = g.astype(jnp.bfloat16).astype(jnp.float32)
    g_parts = (g_high + pltpu.roll(g - g_high, LOW, 1)).astype(jnp.bfloat16)

    scale = math.log2(math.e) * head_size ** (-0.5)

    def project(base, rows):
        at = pl.ds(base, rows)
        block = hidden[at, :]
        q = (dot(block, w_query[...]) * scale).astype(jnp.bfloat16)
        for h in range(HEADS):
            queries[h, at, :] = q[:, h * head_size : (h + 1) * head_size]
        k = dot(block, w_key[...]).astype(jnp.bfloat16)
        for h in range(HEADS):
            keys[h, at, :] = k[:, h * head_size : (h + 1) * head_size]
        v = dot(block, g_parts)
        v = jnp.where(lane < HEADS, v + pltpu.roll(v, LANES - LOW, 1), 0.0)
        v_high = v.astype(jnp.bfloat16).astype(jnp.float32)
        sides[at, :LANES] = (v_high + pltpu.roll(v - v_high, LOW, 1)).astype(jnp.bfloat16)
        sides[at, LANES:] = jnp.ones((rows, LANES), jnp.bfloat16)
        total[at, :] = fold_lanes(block.astype(jnp.float32) * w_score[...])

    loads[5].wait()
    loads[6].wait()
    for base in range(0, local, step):
        project(base, step)

    @pl.when(has_upper)
    def _():
        rows_down().wait_recv()

    @pl.when(has_lower)
    def _():
        rows_down().wait_send()

    pointwise(local, SPILL, x_next[...])
    project(local, SPILL)

    def attend(h, base, rows):
        reach = MAXC - TILE
        low = max(0, base - reach) // SPILL * SPILL
        high = min(rows_all, -(-(base + rows + reach) // SPILL) * SPILL)
        at, span = pl.ds(base, rows), pl.ds(low, high - low)
        q = jnp.concatenate([queries[h, at, :], q_mark[at, :]], axis=1)
        k = jnp.concatenate([keys[h, span, :], k_mark[span, :]], axis=1)
        s = dot_t(q, k)
        p = jnp.exp2(s - jnp.max(s, axis=1, keepdims=True)).astype(jnp.bfloat16)
        o = dot(p, sides[span, :])
        mine = (lane == h) | (lane == h + LOW)
        total[at, :] += jnp.where(mine, o[:, :LANES] / o[:, LANES:], 0.0)

    def scores(base, rows):
        value = jnp.sum(total[pl.ds(base, rows), :].T, axis=0, keepdims=True)
        place = base + lax.broadcasted_iota(jnp.int32, (1, rows), 1)
        live = place < 0
        for j in range(reqs):
            row = starts[j] * TILE
            live = live | ((place >= row) & (place < row + counts[j]))
        return jnp.where(live, value, 0.0), place

    def over_spill(h, carry):
        attend(h, local, SPILL)
        return carry

    lax.fori_loop(0, HEADS, over_spill, 0)
    value, _ = scores(local, SPILL)
    score_out[...] = jnp.broadcast_to(value, score_out.shape)

    @pl.when(has_upper)
    def _():
        score_up().start()

    def over_own(h, carry):
        for base in range(0, local, step):
            attend(h, base, step)
        return carry

    lax.fori_loop(0, HEADS, over_own, 0)
    value, place = scores(0, local)
    out[...] = value

    @pl.when(has_lower)
    def _():
        score_up().wait_recv()

    @pl.when(has_upper)
    def _():
        score_up().wait_send()

    out[:, :SPILL] = jnp.where(
        place[:, :SPILL] < starts[0] * TILE, score_in[0:1, :], value[:, :SPILL]
    )


def per_device(
    shards,
    cand_rows,
    user_rows,
    counts,
    starts,
    norm_gain,
    w_cand,
    w_user,
    w_query,
    w_key,
    w_value,
    w_out,
    w_score,
):
    local, width = cand_rows.shape
    rows_all = local + SPILL
    weight = pltpu.VMEM((width, width), jnp.bfloat16)
    in_smem = pl.BlockSpec(memory_space=pltpu.SMEM)
    in_vmem = pl.BlockSpec(memory_space=pltpu.VMEM)
    anywhere = pl.BlockSpec(memory_space=pl.ANY)
    score = pl.pallas_call(
        functools.partial(kernel, shards),
        out_shape=jax.ShapeDtypeStruct((1, local), jnp.float32),
        in_specs=[in_smem, in_smem, anywhere] + [in_vmem] * 3 + [anywhere] * 6,
        out_specs=in_vmem,
        scratch_shapes=[
            pltpu.VMEM((local, width), jnp.bfloat16),
            pltpu.VMEM((SPILL, width), jnp.bfloat16),
            weight,
            weight,
            weight,
            weight,
            weight,
            weight,
            pltpu.VMEM((LANES, width), jnp.float32),
            pltpu.VMEM((rows_all, width), jnp.bfloat16),
            pltpu.VMEM((HEADS, rows_all, width // HEADS), jnp.bfloat16),
            pltpu.VMEM((HEADS, rows_all, width // HEADS), jnp.bfloat16),
            pltpu.VMEM((rows_all, LANES), jnp.bfloat16),
            pltpu.VMEM((rows_all, LANES), jnp.bfloat16),
            pltpu.VMEM((rows_all, 2 * LANES), jnp.bfloat16),
            pltpu.VMEM((rows_all, LANES), jnp.float32),
            pltpu.VMEM((8, SPILL), jnp.float32),
            pltpu.VMEM((8, SPILL), jnp.float32),
            pltpu.SemaphoreType.DMA((7,)),
            pltpu.SemaphoreType.DMA((2,)),
            pltpu.SemaphoreType.DMA((2,)),
        ],
        compiler_params=pltpu.CompilerParams(
            collective_id=0, has_side_effects=True, vmem_limit_bytes=56 * 1024 * 1024
        ),
        name="rank",
    )(
        starts,
        counts,
        cand_rows,
        user_rows,
        norm_gain[None, :],
        w_score[None, :],
        w_user,
        w_cand,
        w_out,
        w_value,
        w_query,
        w_key,
    )
    return score.reshape(local)


def solution(mesh):
    rows = P(("groups", "cand"))
    wide = P(("groups", "cand"), None)
    return jax.shard_map(
        functools.partial(per_device, mesh.shape["cand"]),
        mesh=mesh,
        in_specs=(wide, wide, rows, rows) + (P(),) * 8,
        out_specs=rows,
        check_vma=False,
    )
```

time: 99.7 us -> 33.5 us (0.34)
  matrix products: 42 us -> 0 us
  Pallas kernels: 0 us -> 32 us
  local copies, waits for them, and re-layouts: 18.3 us -> 0 us
  other arithmetic: 13.9 us -> 1.29 us
  starting transfers between devices: 9.87 us -> 0 us
  waiting for transfers between devices: 9.05 us -> 0 us
  loops' own time: 5.36 us -> 0 us
    dot_general x23 -> x0, matrix products: 42 us -> none  [the longest x8 15.6 us: one_head(): lax.dot_general(q_part, k_part, (((1,), (1,)), ((), ())), preferred_eleme...]
    pallas_call x0 -> x1, Pallas kernels: none -> 32 us  [per_device(): pl.pallas_call(functools.partial(kernel, shards), out_shape=jax.ShapeDtyp...]
    ppermute x4 -> x0, starting transfers between devices: 9.87 us -> none  [passed_along(): return lax.ppermute(block, axis, route)]
    ppermute x4 -> x0, waiting for transfers between devices: 9.05 us -> none  [passed_along(): return lax.ppermute(block, axis, route)]
    dynamic_update_slice x16 -> x0, local copies, waits for them, and re-layouts: 7.1 us -> none  [attend(): mixture = lax.map(one_head, jnp.arange(head_count))]
    another operation x1 -> x0, loops' own time: 5.36 us -> none  [attend(): mixture = lax.map(one_head, jnp.arange(head_count))]
    concatenate x3 -> x0, other arithmetic: 4.76 us -> none  [the longest x1 2.24 us: per_device(): jnp.concatenate([queries, from_above[:, :model_width]], axis=0)]
    dynamic_slice x8 -> x0, local copies, waits for them, and re-layouts: 4.66 us -> none  [attend(): mixture = lax.map(one_head, jnp.arange(head_count))]
  transfers between devices with their start and end apart: 4 -> 0, of which waited for: 4 -> 0; matrix products, arithmetic and copies ran while one was open for 9% -> 0% of each run, Pallas kernels for 0% -> 0%
where the time goes in v1:
time: 33.5 us; the launch traced here: 33.3 us
  Pallas kernels  32 us (96%)
  other arithmetic  1.29 us (4%)
    pallas_call x1, Pallas kernels, per_device(): pl.pallas_call(functools.partial(kernel, shards), out_shape=jax.ShapeDtyp...  32 us
    pallas_call x1, other arithmetic, per_device(): pl.pallas_call(functools.partial(kernel, shards), out_shape=jax.ShapeDtyp...  1.29 us

profile of v1, /device:TPU:24, one launch (start us, length us, event | category | flops | bytes accessed | tf_op | source)
XLA Modules:
  0.0 33.3 jit_solution(9384449800199382031)
XLA Ops:
  0.0 32.0 %rank.1 = f32[1,768]{1,0:T(1,128)} custom-call(s32[6]{0:T(128)} %starts.1, s32[6]{0:T(128)} %counts.1, bf16[768,1024]{1,0:T(8,128)(2,1)} %x_hbm.1, bf16[6,1024]{1,0:T(8,128)(2,1)} %users.1, f32[1,1024]{1,0:T(1,128)} %bitcast.2, f32[1,1024]{1,0:T(1,128)} %bitcast.3, bf16[1024,1024]{1,0:T(8,128)(2,1)} %w_user_hbm.1, bf16[1024,1024]{1,0:T(8,128)(2,1)} %w_cand_hbm.1, ...), custom_call_target="tpu_custom_call" | custom-call | tf_op jit(solution)/shard_map/rank/pallas_call | solution.py:332
  32.0 1.3 %reduce = f32[768]{0:T(1024)} reduce(f32[1,768]{1,0:T(1,128)} %rank.1, f32[]{:T(128)} %constant.3), dimensions={0}, to_apply=%pallas_call.3.reduce_sub_computation | reduce | bytes 6148 | tf_op jit(solution)/shard_map/rank/pallas_call | solution.py:332

commit v2 on v1

--- a/solution.py
+++ b/solution.py
@@ -15,6 +15,8 @@
 LANES = 128
 FAR = -1e30
 LOW = 16
+WIDE = 256
+SIDES = 32
 MESH = pl.DeviceIdType.MESH
 
 
@@ -64,6 +66,7 @@
     w_query,
     w_key,
     terms,
+    normed,
     hidden,
     queries,
     keys,
@@ -71,6 +74,7 @@
     k_mark,
     sides,
     total,
+    mixed,
     score_out,
     score_in,
     load_sem,
@@ -156,6 +160,17 @@
             lane == LANES - 1, dead, live_f
         ).astype(jnp.bfloat16)
 
+    def normalise(base, rows, x):
+        features = x.astype(jnp.float32)
+        mean_square = jnp.mean(features * features, axis=1, keepdims=True)
+        normed[pl.ds(base, rows), :] = (
+            features * lax.rsqrt(mean_square + 1e-06) * gain[...]
+        ).astype(jnp.bfloat16)
+
+    loads[0].wait()
+    for base in range(0, local, SPILL):
+        normalise(base, SPILL, x_own[pl.ds(base, SPILL), :])
+
     terms[...] = jnp.zeros_like(terms)
     loads[1].wait()
     terms[0:reqs, :] = dot(users[...], w_user[...])
@@ -175,21 +190,20 @@
     def _():
         score_in[...] = jnp.zeros_like(score_in)
 
-    def pointwise(base, rows, x):
-        features = x.astype(jnp.float32)
-        mean_square = jnp.mean(features * features, axis=1, keepdims=True)
-        normed = (features * lax.rsqrt(mean_square + 1e-06) * gain[...]).astype(jnp.bfloat16)
+    def pointwise(base, rows, x_ref):
+        at = pl.ds(base, rows)
         held, _ = marks(base, rows)
-        user = dot(jnp.where(held, 1.0, 0.0).astype(jnp.bfloat16), terms[...].astype(jnp.bfloat16))
-        pre = dot(normed, w_cand[...]) + user
-        silu = pre * (0.5 + 0.5 * jnp.tanh(0.5 * pre))
-        hidden[pl.ds(base, rows), :] = (features + silu).astype(jnp.bfloat16)
-
-    loads[0].wait()
+        held = jnp.where(held, 1.0, 0.0).astype(jnp.bfloat16)
+        for column in range(0, width, WIDE):
+            cut = pl.ds(column, WIDE)
+            pre = dot(normed[at, :], w_cand[:, cut])
+            pre = pre + dot(held, terms[:, cut].astype(jnp.bfloat16))
+            silu = pre * (0.5 + 0.5 * jnp.tanh(0.5 * pre))
+            hidden[at, cut] = (x_ref[:, cut].astype(jnp.float32) + silu).astype(jnp.bfloat16)
+
     loads[2].wait()
     step = 2 * SPILL
-    for base in range(0, local, step):
-        pointwise(base, step, x_own[pl.ds(base, step), :])
+    pointwise(0, local, x_own)
 
     loads[3].wait()
     loads[4].wait()
@@ -220,37 +234,43 @@
 
     scale = math.log2(math.e) * head_size ** (-0.5)
 
-    def project(base, rows):
+    def project(weight, kept, base, rows, factor):
+        at = pl.ds(base, rows)
+        for column in range(0, width, WIDE):
+            value = dot(hidden[at, :], weight[:, pl.ds(column, WIDE)])
+            value = (value * factor if factor else value).astype(jnp.bfloat16)
+            for part in range(0, WIDE, head_size):
+                kept[(column + part) // head_size, at, :] = value[:, part : part + head_size]
+
+    def project_side(base, rows):
         at = pl.ds(base, rows)
         block = hidden[at, :]
-        q = (dot(block, w_query[...]) * scale).astype(jnp.bfloat16)
-        for h in range(HEADS):
-            queries[h, at, :] = q[:, h * head_size : (h + 1) * head_size]
-        k = dot(block, w_key[...]).astype(jnp.bfloat16)
-        for h in range(HEADS):
-            keys[h, at, :] = k[:, h * head_size : (h + 1) * head_size]
         v = dot(block, g_parts)
-        v = jnp.where(lane < HEADS, v + pltpu.roll(v, LANES - LOW, 1), 0.0)
+        v = v.T
+        v = v[:HEADS] + v[LOW : LOW + HEADS]
         v_high = v.astype(jnp.bfloat16).astype(jnp.float32)
-        sides[at, :LANES] = (v_high + pltpu.roll(v - v_high, LOW, 1)).astype(jnp.bfloat16)
-        sides[at, LANES:] = jnp.ones((rows, LANES), jnp.bfloat16)
+        ones = jnp.ones((SIDES - 2 * HEADS, rows), jnp.float32)
+        sides[:, at] = jnp.concatenate([v_high, v - v_high, ones], axis=0).astype(jnp.bfloat16)
         total[at, :] = fold_lanes(block.astype(jnp.float32) * w_score[...])
 
     loads[5].wait()
+    project(w_query, queries, 0, local, scale)
+    project_side(0, local)
+
+    @pl.when(has_upper)
+    def _():
+        rows_down().wait_recv()
+
+    @pl.when(has_lower)
+    def _():
+        rows_down().wait_send()
+
+    normalise(local, SPILL, x_next[...])
+    pointwise(local, SPILL, x_next)
     loads[6].wait()
-    for base in range(0, local, step):
-        project(base, step)
-
-    @pl.when(has_upper)
-    def _():
-        rows_down().wait_recv()
-
-    @pl.when(has_lower)
-    def _():
-        rows_down().wait_send()
-
-    pointwise(local, SPILL, x_next[...])
-    project(local, SPILL)
+    project(w_query, queries, local, SPILL, scale)
+    project(w_key, keys, 0, rows_all, None)
+    project_side(local, SPILL)
 
     def attend(h, base, rows):
         reach = MAXC - TILE
@@ -259,14 +279,19 @@
         at, span = pl.ds(base, rows), pl.ds(low, high - low)
         q = jnp.concatenate([queries[h, at, :], q_mark[at, :]], axis=1)
         k = jnp.concatenate([keys[h, span, :], k_mark[span, :]], axis=1)
-        s = dot_t(q, k)
-        p = jnp.exp2(s - jnp.max(s, axis=1, keepdims=True)).astype(jnp.bfloat16)
-        o = dot(p, sides[span, :])
-        mine = (lane == h) | (lane == h + LOW)
-        total[at, :] += jnp.where(mine, o[:, :LANES] / o[:, LANES:], 0.0)
+        s = dot_t(k, q)
+        p = jnp.exp2(s - jnp.max(s, axis=0, keepdims=True)).astype(jnp.bfloat16)
+        o = dot(sides[:, span], p)
+        row = lax.broadcasted_iota(jnp.int32, (SIDES, rows), 0)
+        mine = (row == h) | (row == h + HEADS)
+        above = jnp.sum(jnp.where(mine, o, 0.0), axis=0, keepdims=True)
+        mixed[h, :, at] = above / o[2 * HEADS : 2 * HEADS + 1, :]
 
     def scores(base, rows):
-        value = jnp.sum(total[pl.ds(base, rows), :].T, axis=0, keepdims=True)
+        at = pl.ds(base, rows)
+        value = jnp.sum(total[at, :].T, axis=0, keepdims=True)
+        for h in range(HEADS):
+            value = value + mixed[h, :, at]
         place = base + lax.broadcasted_iota(jnp.int32, (1, rows), 1)
         live = place < 0
         for j in range(reqs):
@@ -274,11 +299,14 @@
             live = live | ((place >= row) & (place < row + counts[j]))
         return jnp.where(live, value, 0.0), place
 
-    def over_spill(h, carry):
-        attend(h, local, SPILL)
+    def both_kinds(i, carry):
+        attend(2 * i, local, SPILL)
+        attend(2 * i + 1, local, SPILL)
+        for base in range(0, local, step):
+            attend(i, base, step)
         return carry
 
-    lax.fori_loop(0, HEADS, over_spill, 0)
+    lax.fori_loop(0, HEADS // 2, both_kinds, 0)
     value, _ = scores(local, SPILL)
     score_out[...] = jnp.broadcast_to(value, score_out.shape)
 
@@ -286,14 +314,14 @@
     def _():
         score_up().start()
 
-    def over_own(h, carry):
+    def own_only(i, carry):
         for base in range(0, local, step):
-            attend(h, base, step)
+            attend(HEADS // 2 + 2 * i, base, step)
+            attend(HEADS // 2 + 2 * i + 1, base, step)
         return carry
 
-    lax.fori_loop(0, HEADS, over_own, 0)
+    lax.fori_loop(0, HEADS // 4, own_only, 0)
     value, place = scores(0, local)
-    out[...] = value
 
     @pl.when(has_lower)
     def _():
@@ -303,9 +331,8 @@
     def _():
         score_up().wait_send()
 
-    out[:, :SPILL] = jnp.where(
-        place[:, :SPILL] < starts[0] * TILE, score_in[0:1, :], value[:, :SPILL]
-    )
+    head = jnp.where(place[:, :SPILL] < starts[0] * TILE, score_in[0:1, :], value[:, :SPILL])
+    out[...] = jnp.concatenate([head, value[:, SPILL:]], axis=1)[0]
 
 
 def per_device(
@@ -329,9 +356,9 @@
     in_smem = pl.BlockSpec(memory_space=pltpu.SMEM)
     in_vmem = pl.BlockSpec(memory_space=pltpu.VMEM)
     anywhere = pl.BlockSpec(memory_space=pl.ANY)
-    score = pl.pallas_call(
+    return pl.pallas_call(
         functools.partial(kernel, shards),
-        out_shape=jax.ShapeDtypeStruct((1, local), jnp.float32),
+        out_shape=jax.ShapeDtypeStruct((local,), jnp.float32),
         in_specs=[in_smem, in_smem, anywhere] + [in_vmem] * 3 + [anywhere] * 6,
         out_specs=in_vmem,
         scratch_shapes=[
@@ -345,12 +372,14 @@
             weight,
             pltpu.VMEM((LANES, width), jnp.float32),
             pltpu.VMEM((rows_all, width), jnp.bfloat16),
+            pltpu.VMEM((rows_all, width), jnp.bfloat16),
             pltpu.VMEM((HEADS, rows_all, width // HEADS), jnp.bfloat16),
             pltpu.VMEM((HEADS, rows_all, width // HEADS), jnp.bfloat16),
             pltpu.VMEM((rows_all, LANES), jnp.bfloat16),
             pltpu.VMEM((rows_all, LANES), jnp.bfloat16),
-            pltpu.VMEM((rows_all, 2 * LANES), jnp.bfloat16),
+            pltpu.VMEM((SIDES, rows_all), jnp.bfloat16),
             pltpu.VMEM((rows_all, LANES), jnp.float32),
+            pltpu.VMEM((HEADS, 1, rows_all), jnp.float32),
             pltpu.VMEM((8, SPILL), jnp.float32),
             pltpu.VMEM((8, SPILL), jnp.float32),
             pltpu.SemaphoreType.DMA((7,)),
@@ -375,7 +404,6 @@
         w_query,
         w_key,
     )
-    return score.reshape(local)
 
 
 def solution(mesh):

time: 33.5 us -> 32.7 us (0.976)
  other arithmetic: 1.29 us -> 0 us
  local copies, waits for them, and re-layouts: 0 us -> 1.28 us
  Pallas kernels: 32 us -> 31.3 us
    pallas_call x1 -> x0, other arithmetic: 1.29 us -> none  [per_device(): pl.pallas_call(functools.partial(kernel, shards), out_shape=jax.ShapeDtyp...]
    unnamed x0 -> x1, local copies, waits for them, and re-layouts: none -> 1.28 us
    pallas_call x1, Pallas kernels: 32 us -> 31.3 us  [per_device(): pl.pallas_call(functools.partial(kernel, shards), out_shape=jax.ShapeDtyp...]
where the time goes in v2:
time: 32.7 us; the launch traced here: 32.5 us
  Pallas kernels  31.3 us (96%)
  local copies, waits for them, and re-layouts  1.28 us (4%)
    pallas_call x1, Pallas kernels, per_device(): pl.pallas_call(functools.partial(kernel, shards), out_shape=jax.ShapeDtyp...  31.3 us
    unnamed x1, local copies, waits for them, and re-layouts  1.28 us

profile of v2, /device:TPU:24, one launch (start us, length us, event | category | flops | bytes accessed | tf_op | source)
XLA Modules:
  0.0 32.5 jit_solution(17615789572698980052)
XLA Ops:
  0.0 31.3 %rank.1 = f32[768]{0:T(1024)} custom-call(s32[6]{0:T(128)} %starts.1, s32[6]{0:T(128)} %counts.1, bf16[768,1024]{1,0:T(8,128)(2,1)} %x_hbm.1, bf16[6,1024]{1,0:T(8,128)(2,1)} %users.1, f32[1,1024]{1,0:T(1,128)} %bitcast.2, f32[1,1024]{1,0:T(1,128)} %bitcast.3, bf16[1024,1024]{1,0:T(8,128)(2,1)} %w_user_hbm.1, bf16[1024,1024]{1,0:T(8,128)(2,1)} %w_cand_hbm.1, ...), custom_call_target="tpu_custom_call" | custom-call | tf_op jit(solution)/shard_map/rank/pallas_call | solution.py:359
  31.3 1.3 %copy.14 = f32[768]{0:T(1024)} copy(f32[768]{0:T(1024)} %rank.1) | data formatting | bytes 6144
